TPU v7x, 32 devices: a whole 2x2x4 slice. The times are simulated.
32 devices in a mesh: group: 2 (over y), role: 2 (over core), tensor: 8 (over z, x).
Axes of the slice: x: 2, y: 2, z: 4, core: 2. Of those that a mesh axis runs over, the one named last changes fastest.
Arguments:
- tokens: bfloat16 [2, 16, 16384], P(None, ('group', 'tensor')), parts along dimension 1, may hold values from -6 to 6
- norm_gain: float32 [16384], replicated, may hold values from 0.1 to 1.9
- w_query: bfloat16 [16384, 1024], P(None, 'tensor'), may hold values from -0.046875 to 0.046875
- w_keyval: bfloat16 [16384, 1024], P(None, 'tensor'), may hold values from -0.046875 to 0.046875
- w_out: bfloat16 [1024, 16384], P('tensor'), may hold values from -0.5 to 0.5
- kv_cache: bfloat16 [16, 512, 1024], P(('group', 'tensor')), parts along dimension 0
- cache_len: int32 [16], P(('group', 'tensor')), parts along dimension 0, may hold values from 1 to 512, as said below
- prompt_kv: bfloat16 [2, 32, 128, 1024], P('role', ('group', 'tensor')), parts along dimension 1, may hold values from -6 to 6
- block_owner: int32 [2, 32, 1], P(None, 'group'), parts along dimension 1, may hold values from 0 to 7; in each aligned block of 16 rows (0 to 15, 16 to 31, ..., all dimensions but the last counted through in order) at most 4 rows name the same one
- block_tokens: int32 [2, 32], P(None, 'group'), parts along dimension 1, may hold values from 1 to 128
Outputs:
- attended: bfloat16 [2, 16, 16384], P(None, ('group', 'tensor')), parts along dimension 1
- landed: bfloat16 [2, 64, 128, 1024], P('role', ('group', 'tensor')), parts along dimension 1
There are 2 independent parts, one for each index of `group`. A program takes and returns all parts, laid end to end along the dimension named above; an argument that names none is the same for every part. Nothing has to cross between parts.
Inputs may be any that keep to these rules, and one draw needn't show every extreme that they name: `block_owner`: within each side's 16 blocks no owner receives more than 4 blocks, and some owner receives exactly 4. `cache_len`: some decode row has all 512 positions live.
All inputs are finite; a program needn't handle non-finite values.
Results may differ from a plain program's by a relative error of at most 0.0081.
Values may be sent and summed in bfloat16 or wider, within the bound.
A program may use at most 192 MiB of HBM per device.

v0:
```python
import jax
import jax.numpy as jnp
from jax import lax
from jax.sharding import PartitionSpec as P

HEAD = 128
KVH = 4
STEPS = 2
ROWS = 1
CAP = 4
KVW = 1024


def norm_rows(row_values, norm_gain):
    as_float = row_values.astype(jnp.float32)
    factor = lax.rsqrt(jnp.mean(as_float * as_float, axis=-1, keepdims=True) + 1e-05)
    return (as_float * factor * norm_gain).astype(jnp.bfloat16)


def owner_ranks(owner_ids, owner_total):
    owner_hits = (owner_ids[:, None] == jnp.arange(owner_total, dtype=jnp.int32)[None, :]).astype(
        jnp.int32
    )
    return jnp.sum(jnp.cumsum(owner_hits, axis=0) * owner_hits, axis=1) - 1


def place_pages(blocks, owners, ranks, own_index, capacity):
    block_count = blocks.shape[0]
    chosen = (owners == own_index)[:, None] & (
        ranks[:, None] == jnp.arange(capacity, dtype=jnp.int32)[None, :]
    )
    placing = chosen.astype(jnp.bfloat16)
    flattened = blocks.reshape(block_count, -1)
    pages = jnp.einsum("jc,jf->cf", placing, flattened, preferred_element_type=jnp.float32)
    return pages.astype(jnp.bfloat16).reshape((capacity,) + blocks.shape[1:])


def attend(queries, kv_cache, cache_len, fresh_kv):
    row_count, head_count, head_width = queries.shape
    group_size = head_count // KVH
    key_width = KVH * head_width
    q_heads = queries.reshape(row_count, KVH, group_size, head_width)
    cache_keys = kv_cache[:, :, :key_width].reshape(row_count, -1, KVH, head_width)
    cache_vals = kv_cache[:, :, key_width:].reshape(row_count, -1, KVH, head_width)
    fresh_keys = fresh_kv[:, :, :key_width].reshape(row_count, -1, KVH, head_width)
    fresh_vals = fresh_kv[:, :, key_width:].reshape(row_count, -1, KVH, head_width)
    score_scale = 1.0 / head_width**0.5
    cache_scores = (
        jnp.einsum("rkgd,rpkd->rkgp", q_heads, cache_keys, preferred_element_type=jnp.float32)
        * score_scale
    )
    live_mask = jnp.arange(kv_cache.shape[1], dtype=jnp.int32)[None, :] < cache_len[:, None]
    cache_scores = jnp.where(live_mask[:, None, None, :], cache_scores, jnp.float32(-1e30))
    fresh_scores = (
        jnp.einsum("rkgd,rpkd->rkgp", q_heads, fresh_keys, preferred_element_type=jnp.float32)
        * score_scale
    )
    largest = jnp.maximum(jnp.max(cache_scores, axis=-1), jnp.max(fresh_scores, axis=-1))[..., None]
    cache_exp = jnp.exp(cache_scores - largest)
    fresh_exp = jnp.exp(fresh_scores - largest)
    denominator = jnp.sum(cache_exp, axis=-1, keepdims=True) + jnp.sum(
        fresh_exp, axis=-1, keepdims=True
    )
    cache_weights = (cache_exp / denominator).astype(jnp.bfloat16)
    fresh_weights = (fresh_exp / denominator).astype(jnp.bfloat16)
    combined = jnp.einsum(
        "rkgp,rpkd->rkgd", cache_weights, cache_vals, preferred_element_type=jnp.float32
    )
    combined = combined + jnp.einsum(
        "rkgp,rpkd->rkgd", fresh_weights, fresh_vals, preferred_element_type=jnp.float32
    )
    return combined.reshape(row_count, head_count * head_width).astype(jnp.bfloat16)


def body(
    tokens,
    norm_gain,
    w_query,
    w_keyval,
    w_out,
    kv_cache,
    cache_len,
    prompt_kv,
    block_owner,
    block_tokens,
):
    owner_total = lax.axis_size("tensor")
    role_index = lax.axis_index("role")
    tensor_index = lax.axis_index("tensor")
    local_count = prompt_kv.shape[1]
    tile_size = prompt_kv.shape[2]
    side_owner = lax.dynamic_index_in_dim(block_owner[:, :, 0], role_index, 0, keepdims=False)
    side_tokens = lax.dynamic_index_in_dim(block_tokens, role_index, 0, keepdims=False)
    side_ranks = owner_ranks(side_owner, owner_total)
    first_block = tensor_index * local_count
    local_owner = lax.dynamic_slice_in_dim(side_owner, first_block, local_count, 0)
    local_tokens = lax.dynamic_slice_in_dim(side_tokens, first_block, local_count, 0)
    token_mask = jnp.arange(tile_size, dtype=jnp.int32)[None, :] < local_tokens[:, None]
    masked = jnp.where(token_mask[:, :, None], prompt_kv[0], jnp.zeros((), prompt_kv.dtype))
    destination = (
        jnp.arange(owner_total, dtype=jnp.int32)[:, None, None, None]
        == local_owner[None, :, None, None]
    )
    outgoing = jnp.where(destination, masked[None], jnp.zeros((), masked.dtype))
    arrived = lax.all_to_all(outgoing, "tensor", split_axis=0, concat_axis=0, tiled=True)
    arrived = arrived.reshape((-1,) + masked.shape[1:])
    own_pages = place_pages(arrived, side_owner, side_ranks, tensor_index, CAP)
    landed = own_pages[None]
    row_count = ROWS
    fresh_list = []
    results = []
    for step_index in range(STEPS):
        normed = norm_rows(tokens[step_index], norm_gain)
        shard_rows = lax.all_gather(normed, "tensor", axis=0, tiled=True)
        query_part = jnp.dot(shard_rows, w_query, preferred_element_type=jnp.float32)
        keyval_part = jnp.dot(shard_rows, w_keyval, preferred_element_type=jnp.float32)
        projected = jnp.concatenate([query_part, keyval_part], axis=1).astype(jnp.bfloat16)
        owned = lax.all_to_all(
            projected, "tensor", split_axis=0, concat_axis=1, tiled=True
        ).reshape(row_count, owner_total, -1)
        queries = owned[:, :, :HEAD]
        fresh_list.append(owned[:, :, HEAD:].reshape(row_count, 1, KVW))
        fresh_kv = jnp.concatenate(fresh_list, axis=1)
        heads_out = attend(queries, kv_cache, cache_len, fresh_kv)
        head_slices = lax.all_to_all(heads_out, "tensor", split_axis=1, concat_axis=0, tiled=True)
        summed = lax.psum_scatter(
            jnp.dot(head_slices, w_out, preferred_element_type=jnp.float32),
            "tensor",
            scatter_dimension=0,
            tiled=True,
        )
        results.append(summed.astype(jnp.bfloat16))
    stacked = jnp.stack(results)
    return (stacked, landed)


def solution(mesh):
    in_specs = (
        P(None, ("group", "tensor"), None),
        P(),
        P(None, "tensor"),
        P(None, "tensor"),
        P("tensor", None),
        P(("group", "tensor"), None, None),
        P(("group", "tensor")),
        P("role", ("group", "tensor"), None, None),
        P(None, "group", None),
        P(None, "group"),
    )
    out_specs = (P(None, ("group", "tensor"), None), P("role", ("group", "tensor"), None, None))
    return jax.shard_map(body, mesh=mesh, in_specs=in_specs, out_specs=out_specs, check_vma=False)
```

profile of v0, /device:TPU:0, one launch (start us, length us, event | category | flops | bytes accessed | tf_op | source)
XLA Modules:
  0.0 275.5 jit_solution(3578399213950149163)
XLA Ops:
  0.6 1.7 multiply_reduce_fusion.1
  3.7 1.0 convert_multiply_fusion.1
  4.8 0.9 multiply_convert_fusion.1
  5.6 32.5 %all-gather = bf16[131072]{0:T(1024)(128)(2,1)S(1)} all-gather(bf16[16384]{0:T(1024)(128)(2,1)S(1)} %get-tuple-element.10), channel_id=2, replica_groups=mesh['group'=2,'role'=2,'tensor'=8] {'tensor'}, dimensions={0}, use_global_device_ids=true | all-gather | bytes 294912 | tf_op jit(solution)/shard_map/all_gather | solution.py:114
  38.3 3.0 %fusion.5 = bf16[8,1,128]{2,0,1:T(8,128)(2,1)S(1)} fusion(bf16[8,16384]{1,0:T(8,128)(2,1)S(1)} %reshape.448, bf16[16384,128]{1,0:T(8,128)(2,1)} %param.13), kind=kOutput, calls=%fused_computation.16 | convolution fusion | flops 33555456 | bytes 4458496 | tf_op jit(solution)/shard_map/dot_general | solution.py:116
  41.3 0.4 copy-done.1
  41.7 0.6 fusion.4
  42.4 0.5 broadcast.116
  42.9 0.6 reduce.17
  43.6 0.6 reshape.457
  44.2 5.5 %all-to-all-start = ((bf16[8,2,128]{2,1,0:T(2,128)(2,1)}), bf16[8,2,128]{2,1,0:T(2,128)(2,1)S(1)}, u32[]{:S(2)}, u32[]{:S(2)}) async-start(bf16[8,2,128]{2,1,0:T(2,128)(2,1)} %reshape.457), calls=%async_computation | async-start | bytes 8192 | tf_op jit(solution)/shard_map/all_to_all | solution.py:118
  49.7 31.3 %all-gather.1 = bf16[131072]{0:T(1024)(128)(2,1)S(1)} all-gather(bf16[16384]{0:T(1024)(128)(2,1)S(1)} %get-tuple-element.11), channel_id=3, replica_groups=mesh['group'=2,'role'=2,'tensor'=8] {'tensor'}, dimensions={0}, use_global_device_ids=true | all-gather | bytes 294912 | tf_op jit(solution)/shard_map/all_gather | solution.py:114
  81.1 3.0 %fusion.7 = bf16[8,1,128]{2,0,1:T(8,128)(2,1)S(1)} fusion(bf16[8,16384]{1,0:T(8,128)(2,1)S(1)} %reshape.449, bf16[16384,128]{1,0:T(8,128)(2,1)} %param.13), kind=kOutput, calls=%fused_computation.18 | convolution fusion | flops 33555456 | bytes 4458496 | tf_op jit(solution)/shard_map/dot_general | solution.py:116
  84.1 0.4 copy-done.2
  84.5 0.6 fusion.6
  86.3 0.7 reduce.16
  87.0 0.6 reshape.455
  87.6 0.2 copy.53
  87.8 0.2 copy.54
  88.0 5.5 %all-to-all-start.2 = ((bf16[8,2,128]{2,1,0:T(2,128)(2,1)}), bf16[8,2,128]{2,1,0:T(2,128)(2,1)S(1)}, u32[]{:S(2)}, u32[]{:S(2)}) async-start(bf16[8,2,128]{2,1,0:T(2,128)(2,1)} %reshape.455), calls=%async_computation.2 | async-start | bytes 8192 | tf_op jit(solution)/shard_map/all_to_all | solution.py:118
  93.6 0.1 fusion.37
  93.7 6.2 %all-to-all-done.2 = bf16[8,2,128]{2,1,0:T(2,128)(2,1)S(1)} async-done(((bf16[8,2,128]{2,1,0:T(2,128)(2,1)}), bf16[8,2,128]{2,1,0:T(2,128)(2,1)S(1)}, u32[]{:S(2)}, u32[]{:S(2)}) %all-to-all-start.2) | async-done | bytes 4128 | tf_op jit(solution)/shard_map/all_to_all | solution.py:118
  100.0 0.3 fusion.47
  100.2 0.3 fusion.45
  100.5 0.1 fusion.46
  100.7 0.2 fusion.10
  100.9 0.2 fusion.11
  101.1 0.3 fusion.12
  101.3 0.2 fusion.3
  101.6 0.6 copy.41
  102.2 3.3 %all-to-all-start.3 = ((bf16[1,8,128]{2,0,1:T(2,128)(2,1)}), bf16[1,8,128]{2,0,1:T(2,128)(2,1)S(1)}, u32[]{:S(2)}, u32[]{:S(2)}) async-start(bf16[1,8,128]{2,0,1:T(2,128)(2,1)} %copy.41), calls=%async_computation.3 | async-start | bytes 8192 | tf_op jit(solution)/shard_map/all_to_all | solution.py:125
  105.5 0.3 fusion.2
  105.8 0.6 copy.36
  106.4 5.4 %all-to-all-done.3 = bf16[1,8,128]{2,0,1:T(2,128)(2,1)S(1)} async-done(((bf16[1,8,128]{2,0,1:T(2,128)(2,1)}), bf16[1,8,128]{2,0,1:T(2,128)(2,1)S(1)}, u32[]{:S(2)}, u32[]{:S(2)}) %all-to-all-start.3) | async-done | bytes 2080 | tf_op jit(solution)/shard_map/all_to_all | solution.py:125
  111.8 3.3 %all-to-all-start.1 = ((bf16[1,8,128]{2,0,1:T(2,128)(2,1)}), bf16[1,8,128]{2,0,1:T(2,128)(2,1)S(1)}, u32[]{:S(2)}, u32[]{:S(2)}) async-start(bf16[1,8,128]{2,0,1:T(2,128)(2,1)} %copy.36), calls=%async_computation.1 | async-start | bytes 8192 | tf_op jit(solution)/shard_map/all_to_all | solution.py:125
  115.1 2.4 broadcast_select_fusion
  117.5 7.5 %all-to-all-done.1 = bf16[1,8,128]{2,0,1:T(2,128)(2,1)S(1)} async-done(((bf16[1,8,128]{2,0,1:T(2,128)(2,1)}), bf16[1,8,128]{2,0,1:T(2,128)(2,1)S(1)}, u32[]{:S(2)}, u32[]{:S(2)}) %all-to-all-start.1) | async-done | bytes 2080 | tf_op jit(solution)/shard_map/all_to_all | solution.py:125
  125.0 8.1 %all-to-all-start.4 = ((bf16[8,2,128,1024]{3,2,1,0:T(8,128)(2,1)}), bf16[8,2,128,1024]{3,2,1,0:T(8,128)(2,1)}, u32[]{:S(2)}, u32[]{:S(2)}) async-start(bf16[8,2,128,1024]{3,2,1,0:T(8,128)(2,1)} %broadcast_select_fusion), calls=%async_computation.4 | async-start | bytes 8388608 | tf_op jit(solution)/shard_map/all_to_all | solution.py:105
  133.2 0.6 dynamic-slice.4
  133.8 0.2 select_reduce_fusion
  134.0 3.2 %fusion.30 = f32[8,16384]{1,0:T(8,128)S(1)} fusion(bf16[128,16384]{1,0:T(8,128)(2,1)} %param.14, bf16[1,8,128]{2,0,1:T(2,128)(2,1)S(1)} %all-to-all-done.1), kind=kOutput, calls=%fused_computation.69 | convolution fusion | flops 33554432 | bytes 4720640 | tf_op jit(solution)/shard_map/dot_general | solution.py:127
  137.2 0.7 fusion.27
  137.9 129.0 %all-reduce.4 = (bf16[8,16384]{1,0:T(8,128)(2,1)S(1)}, bf16[8,16384]{1,0:T(8,128)(2,1)S(1)}) all-reduce(f32[8,16384]{1,0:T(8,128)S(1)} %fusion.27, f32[8,16384]{1,0:T(8,128)S(1)} %fusion.30), channel_id=5, replica_groups=mesh['group'=2,'role'=2,'tensor'=8] {'tensor'}, use_global_device_ids=true, to_apply=%region_9.10.clone | all-reduce | flops 262144 | bytes 1572864
  266.9 0.8 fusion.8
  267.7 0.8 pad_maximum_fusion
  268.5 4.5 %copy.55 = bf16[2,8,128,1024]{3,1,2,0:T(8,128)(2,1)S(1)} copy(bf16[2,8,128,1024]{3,2,1,0:T(8,128)(2,1)} %bitcast.31) | data formatting | bytes 8388608
  273.0 1.2 convolution_convert_fusion
  274.2 1.3 copy.68
  (45 shorter events, 1.0 us)
Async XLA Ops:
  0.6 85.2 %copy-start = (s32[2,16]{1,0:T(2,128)S(1)}, s32[2,16]{1,0:T(2,128)}, u32[]{:S(2)}) copy-start(s32[2,16]{1,0:T(2,128)} %param.19) | copy-start | bytes 388
  38.3 3.5 %copy-start.1 = (bf16[16384,128]{1,0:T(8,128)(2,1)S(1)}, bf16[16384,128]{1,0:T(8,128)(2,1)}, u32[]{:S(2)}) copy-start(bf16[16384,128]{1,0:T(8,128)(2,1)} %param.12) | copy-start | bytes 12582916
  44.2 43.9 %all-to-all-start = ((bf16[8,2,128]{2,1,0:T(2,128)(2,1)}), bf16[8,2,128]{2,1,0:T(2,128)(2,1)S(1)}, u32[]{:S(2)}, u32[]{:S(2)}) async-start(bf16[8,2,128]{2,1,0:T(2,128)(2,1)} %reshape.457), calls=%async_computation | async-start | bytes 8192 | tf_op jit(solution)/shard_map/all_to_all | solution.py:118
  81.1 3.5 %copy-start.2 = (bf16[16384,128]{1,0:T(8,128)(2,1)S(1)}, bf16[16384,128]{1,0:T(8,128)(2,1)}, u32[]{:S(2)}) copy-start(bf16[16384,128]{1,0:T(8,128)(2,1)} %param.12) | copy-start | bytes 12582916
  81.1 4.8 %copy-start.6 = (s32[2,16,1]{1,2,0:T(1,128)S(1)}, s32[2,16,1]{1,2,0:T(1,128)}, u32[]{:S(2)}) copy-start(s32[2,16,1]{1,2,0:T(1,128)} %param.18) | copy-start | bytes 388
  81.1 5.0 %copy-start.4 = (bf16[1,512,1024]{2,1,0:T(8,128)(2,1)S(1)}, bf16[1,512,1024]{2,1,0:T(8,128)(2,1)}, u32[]{:S(2)}) copy-start(bf16[1,512,1024]{2,1,0:T(8,128)(2,1)} %param.15) | copy-start | bytes 3145732
  84.5 1.7 copy-start.5
  88.0 11.9 %all-to-all-start.2 = ((bf16[8,2,128]{2,1,0:T(2,128)(2,1)}), bf16[8,2,128]{2,1,0:T(2,128)(2,1)S(1)}, u32[]{:S(2)}, u32[]{:S(2)}) async-start(bf16[8,2,128]{2,1,0:T(2,128)(2,1)} %reshape.455), calls=%async_computation.2 | async-start | bytes 8192 | tf_op jit(solution)/shard_map/all_to_all | solution.py:118
  102.2 9.6 %all-to-all-start.3 = ((bf16[1,8,128]{2,0,1:T(2,128)(2,1)}), bf16[1,8,128]{2,0,1:T(2,128)(2,1)S(1)}, u32[]{:S(2)}, u32[]{:S(2)}) async-start(bf16[1,8,128]{2,0,1:T(2,128)(2,1)} %copy.41), calls=%async_computation.3 | async-start | bytes 8192 | tf_op jit(solution)/shard_map/all_to_all | solution.py:125
  111.8 13.2 %all-to-all-start.1 = ((bf16[1,8,128]{2,0,1:T(2,128)(2,1)}), bf16[1,8,128]{2,0,1:T(2,128)(2,1)S(1)}, u32[]{:S(2)}, u32[]{:S(2)}) async-start(bf16[1,8,128]{2,0,1:T(2,128)(2,1)} %copy.36), calls=%async_computation.1 | async-start | bytes 8192 | tf_op jit(solution)/shard_map/all_to_all | solution.py:125
  117.5 15.7 %copy-start.7 = (u32[32]{0:T(128)S(1)}, u32[32]{0:T(128)}, u32[]{:S(2)}) copy-start(u32[32]{0:T(128)} %constant.86) | copy-start | bytes 388
  125.0 143.5 %all-to-all-start.4 = ((bf16[8,2,128,1024]{3,2,1,0:T(8,128)(2,1)}), bf16[8,2,128,1024]{3,2,1,0:T(8,128)(2,1)}, u32[]{:S(2)}, u32[]{:S(2)}) async-start(bf16[8,2,128,1024]{3,2,1,0:T(8,128)(2,1)} %broadcast_select_fusion), calls=%async_computation.4 | async-start | bytes 8388608 | tf_op jit(solution)/shard_map/all_to_all | solution.py:105
  133.2 4.0 %copy-start.3 = (bf16[128,16384]{1,0:T(8,128)(2,1)S(1)}, bf16[128,16384]{1,0:T(8,128)(2,1)}, u32[]{:S(2)}) copy-start(bf16[128,16384]{1,0:T(8,128)(2,1)} %param.14) | copy-start | bytes 12582916
where the time goes:
time: 276 us; the launch traced here: 275 us
  blocking collectives  193 us (70%)
  starting transfers between devices  25.7 us (9%)
  waiting for transfers between devices  19.1 us (7%)
  matrix products  13.9 us (5%)
  local copies, waits for them, and re-layouts  12 us (4%)
  other arithmetic  8.98 us (3%)
  between operations  2.92 us (1%)
    unnamed x1, blocking collectives  129 us
    all_gather x2, blocking collectives, body(): shard_rows = lax.all_gather(normed, 'tensor', axis=0, tiled=True)  63.8 us
    all_to_all x2, waiting for transfers between devices, body(): lax.all_to_all(heads_out, 'tensor', split_axis=1, concat_axis=0, tiled=True)  12.9 us
    all_to_all x2, starting transfers between devices, body(): lax.all_to_all(projected, 'tensor', split_axis=0, concat_axis=1, tiled=True)  11 us
    unnamed x27, local copies, waits for them, and re-layouts  8.93 us
    all_to_all x1, starting transfers between devices, body(): lax.all_to_all(outgoing, 'tensor', split_axis=0, concat_axis=0, tiled=True)  8.1 us
    all_to_all x2, starting transfers between devices, body(): lax.all_to_all(heads_out, 'tensor', split_axis=1, concat_axis=0, tiled=True)  6.62 us
    all_to_all x2, waiting for transfers between devices, body(): lax.all_to_all(projected, 'tensor', split_axis=0, concat_axis=1, tiled=True)  6.23 us
  transfers between devices with their start and end apart: 5, of which 3 were waited for; matrix products, arithmetic and copies ran while one was open for 6% of the time, Pallas kernels for 0%

commit v1 on v0

v1 whole, which is shorter than its diff:
```python
import functools

import jax
import jax.numpy as jnp
from jax import lax
from jax.experimental import pallas as pl
from jax.experimental.pallas import tpu as pltpu
from jax.sharding import PartitionSpec as P

HEAD = 128
KVH = 4
STEPS = 2
CAP = 4
LANES = 1024
CHUNKS = 8
MESH = pl.DeviceIdType.MESH


def kernel(
    n,
    parts,
    tok_ref,
    gain_ref,
    wq_hbm,
    wkv_hbm,
    wo_hbm,
    cache_hbm,
    len_ref,
    prompt_hbm,
    owner_ref,
    count_ref,
    out_ref,
    landed_hbm,
    wq_v,
    wkv_v,
    wo_v,
    cache_v,
    xg,
    xf,
    pmine,
    ppeer,
    asend,
    arecv,
    hsend,
    hrecv,
    rsend,
    rrecv,
    blk,
    pages,
    res,
    local_sem,
    own_sem,
    pair_send,
    pair_recv,
    x_send,
    x_recv,
    b_send,
    b_recv,
    a_send,
    a_recv,
    h_send,
    h_recv,
    r_send,
    r_recv,
    g_send,
    g_recv,
):
    me = lax.axis_index("tensor")
    role = lax.axis_index("role")
    rows = 2 * n
    kvl = wkv_v.shape[1]
    ctx = cache_v.shape[0]
    key_width = KVH * HEAD
    half_k = CHUNKS * LANES
    slab = blk.shape[2]
    nblocks = owner_ref.shape[1]
    part = lax.rem(me, parts)
    base = me - part

    def local(src, dst, i):
        return pltpu.make_async_copy(src, dst, local_sem.at[i])

    k0 = pl.multiple_of(role * half_k, half_k)
    loads = [
        local(wq_hbm.at[pl.ds(k0, half_k), :], wq_v, 0),
        local(wkv_hbm.at[pl.ds(k0, half_k), :], wkv_v, 1),
        local(cache_hbm.at[0], cache_v, 2),
        local(wo_hbm.at[:, pl.ds(k0, half_k)], wo_v, 3),
        local(
            prompt_hbm.at[0, :, pl.ds(pl.multiple_of(part * slab, slab), slab), :], blk.at[me], 4
        ),
    ]
    for load in loads:
        load.start()

    barrier = pltpu.get_barrier_semaphore()

    def greet(d, carry):
        pl.semaphore_signal(
            barrier, inc=1, device_id={"tensor": lax.rem(me + d, n)}, device_id_type=MESH
        )
        return carry

    pl.semaphore_signal(barrier, inc=1, device_id={"role": 1 - role}, device_id_type=MESH)
    lax.fori_loop(1, n, greet, 0)

    xs = tok_ref[...].astype(jnp.float32).reshape(2, STEPS, CHUNKS, LANES)
    total = jnp.sum(xs * xs, axis=(0, 2), keepdims=True)
    total = jnp.sum(total, axis=3, keepdims=True)
    factor = lax.rsqrt(total[0] * (1.0 / (2 * half_k)) + 1e-05)
    mine = tok_ref[role].astype(jnp.float32).reshape(STEPS, CHUNKS, LANES)
    normed = mine * factor * gain_ref[role][None]
    xg[me] = normed.reshape(STEPS * CHUNKS, LANES).astype(jnp.bfloat16)

    pl.semaphore_wait(barrier, n)

    def remote(src, dst, send, recv, peer):
        return pltpu.make_async_remote_copy(
            src_ref=src,
            dst_ref=dst,
            send_sem=send,
            recv_sem=recv,
            device_id={"tensor": peer},
            device_id_type=MESH,
        )

    def each(action, count=n):
        def step(d, carry):
            action(d)
            return carry

        lax.fori_loop(1, count, step, 0)

    def peer_at(d):
        return lax.rem(me + d, n)

    def x_copy(peer, slot):
        return remote(xg.at[me], xg.at[slot], x_send.at[peer], x_recv.at[slot], peer)

    def b_copy(peer, slot):
        at = pl.multiple_of(lax.rem(peer, parts) * slab, slab)
        return remote(
            prompt_hbm.at[0, :, pl.ds(at, slab), :],
            blk.at[slot],
            b_send.at[peer],
            b_recv.at[slot],
            peer,
        )

    def block_of(ref, i, height):
        return ref.at[pl.ds(pl.multiple_of(i * height, height), height), :]

    def a_copy(peer, slot):
        return remote(
            block_of(asend, peer, 8), block_of(arecv, slot, 8), a_send.at[peer], a_recv.at[slot], peer
        )

    def h_copy(peer, slot):
        return remote(
            block_of(hsend, peer, 8), block_of(hrecv, slot, 8), h_send.at[peer], h_recv.at[slot], peer
        )

    def r_copy(peer, slot):
        return remote(
            block_of(rsend, peer, 16), rrecv.at[slot], r_send.at[peer], r_recv.at[slot], peer
        )

    def group_peer(d):
        return base + lax.rem(part + d, parts)

    def g_copy(peer, slot_part):
        local_peer = lax.rem(peer, parts)
        return remote(
            pages.at[local_peer],
            landed_hbm.at[0, :, pl.ds(pl.multiple_of(slot_part * slab, slab), slab), :],
            g_send.at[local_peer],
            g_recv.at[slot_part],
            peer,
        )

    each(lambda d: x_copy(peer_at(d), me).start())
    each(lambda d: b_copy(peer_at(d), me).start())

    loads[0].wait()
    loads[1].wait()
    each(lambda d: x_copy(peer_at(d), peer_at(d)).wait_recv())
    xf[...] = xg[...].astype(jnp.float32).reshape(rows * CHUNKS, LANES)
    q_part = jnp.zeros((rows, HEAD), jnp.float32)
    kv_part = jnp.zeros((rows, kvl), jnp.float32)
    for c in range(CHUNKS):
        lhs = xf.reshape(rows, CHUNKS, LANES)[:, c, :].astype(jnp.bfloat16)
        span = pl.ds(c * LANES, LANES)
        q_part += jnp.dot(lhs, wq_v[span, :], preferred_element_type=jnp.float32)
        kv_part += jnp.dot(lhs, wkv_v[span, :], preferred_element_type=jnp.float32)
    pmine[:, :HEAD] = q_part
    pmine[:, HEAD : HEAD + kvl] = kv_part
    pair = pltpu.make_async_remote_copy(
        src_ref=pmine,
        dst_ref=ppeer,
        send_sem=pair_send.at[0],
        recv_sem=pair_recv.at[0],
        device_id={"role": 1 - role},
        device_id_type=MESH,
    )
    pair.start()
    pair.wait_recv()
    proj = (q_part + ppeer[:, :HEAD]).astype(jnp.bfloat16).astype(jnp.float32)
    kv_proj = (kv_part + ppeer[:, HEAD : HEAD + kvl]).astype(jnp.bfloat16).astype(jnp.float32)

    spread, spread_next = pl.ds(0, rows, stride=4), pl.ds(1, rows, stride=4)
    if kvl < HEAD:
        blank = jnp.zeros((rows, HEAD - kvl), jnp.float32)
        kv_proj = jnp.concatenate([kv_proj, blank], axis=1)
    asend[spread, :] = proj
    asend[spread_next, :] = kv_proj
    each(lambda d: a_copy(peer_at(d), me).start())
    block_of(arecv, me, 8)[...] = block_of(asend, me, 8)[...]
    loads[2].wait()
    each(lambda d: a_copy(peer_at(d), peer_at(d)).wait_recv())

    qs = arecv[spread, :]
    fresh = arecv[spread_next, :][:, :kvl]
    row_ids = lax.broadcasted_iota(jnp.int32, (rows, 1), 0)
    row_group = row_ids // (2 * (n // KVH))
    late = lax.rem(row_ids, 2) == 1
    per = HEAD // kvl

    def fresh_rows(offset, step):
        picked = jnp.zeros((rows, HEAD), jnp.float32)
        for g in range(KVH):
            pieces = []
            for i in range(per):
                at = 2 * (offset + g * per + i) + step
                pieces.append(fresh[at : at + 1, :])
            piece = pieces[0] if per == 1 else jnp.concatenate(pieces, axis=1)
            picked = jnp.where(row_group == g, piece, picked)
        return picked

    scale = 1.0 / HEAD**0.5
    q_low = qs.astype(jnp.bfloat16)
    scores = jnp.zeros((rows, ctx), jnp.float32)
    for g in range(KVH):
        keys = cache_v[:, g * HEAD : (g + 1) * HEAD]
        part_scores = lax.dot_general(
            q_low, keys, (((1,), (1,)), ((), ())), preferred_element_type=jnp.float32
        )
        scores = jnp.where(row_group == g, part_scores, scores)
    live = lax.broadcasted_iota(jnp.int32, (rows, ctx), 1) < len_ref[0]
    scores = jnp.where(live, scores * scale, jnp.float32(-1e30))
    first = jnp.sum(qs * fresh_rows(0, 0), axis=1, keepdims=True) * scale
    second = jnp.sum(qs * fresh_rows(0, 1), axis=1, keepdims=True) * scale
    second = jnp.where(late, second, jnp.float32(-1e30))
    largest = jnp.maximum(jnp.max(scores, axis=1, keepdims=True), jnp.maximum(first, second))
    cache_exp = jnp.exp(scores - largest)
    first_exp = jnp.exp(first - largest)
    second_exp = jnp.where(late, jnp.exp(second - largest), 0.0)
    denominator = jnp.sum(cache_exp, axis=1, keepdims=True) + first_exp + second_exp
    weights = (cache_exp / denominator).astype(jnp.bfloat16)
    first_weight = (first_exp / denominator).astype(jnp.bfloat16).astype(jnp.float32)
    second_weight = (second_exp / denominator).astype(jnp.bfloat16).astype(jnp.float32)
    values = first_weight * fresh_rows(n // 2, 0) + second_weight * fresh_rows(n // 2, 1)
    for g in range(KVH):
        vals = cache_v[:, key_width + g * HEAD : key_width + (g + 1) * HEAD]
        part_values = jnp.dot(weights, vals, preferred_element_type=jnp.float32)
        values = values + jnp.where(row_group == g, part_values, 0.0)
    heads_out = values.astype(jnp.bfloat16).astype(jnp.float32)

    hsend[spread, :] = heads_out
    each(lambda d: h_copy(peer_at(d), me).start())
    block_of(hrecv, me, 8)[...] = block_of(hsend, me, 8)[...]
    loads[3].wait()
    each(lambda d: h_copy(peer_at(d), peer_at(d)).wait_recv())

    lhs = hrecv[spread, :].astype(jnp.bfloat16)
    for c in range(CHUNKS):
        product = jnp.dot(
            lhs, wo_v[:, c * LANES : (c + 1) * LANES], preferred_element_type=jnp.float32
        )
        rsend.reshape(rows, CHUNKS, LANES)[:, c, :] = product
    each(lambda d: r_copy(peer_at(d), me).start())
    rrecv[me] = block_of(rsend, me, 16)[...]

    loads[4].wait()
    each(lambda d: b_copy(peer_at(d), peer_at(d)).wait_recv())
    slab_rows = lax.broadcasted_iota(jnp.int32, (slab, 1), 0) + part * slab
    for o in range(parts):
        wanted = base + o

        def scan(j, carry):
            hits, found = carry[0], carry[1:]
            hit = owner_ref[role, j] == wanted
            found = tuple(
                jnp.where(hit & (hits == s), j, found[s]) for s in range(CAP)
            )
            return (hits + jnp.where(hit, 1, 0),) + found

        zero = jnp.int32(0)
        scanned = lax.fori_loop(0, nblocks, scan, (zero,) * (1 + CAP))
        for s in range(CAP):
            at = scanned[1 + s]
            limit = jnp.where(scanned[0] > s, count_ref[role, at], 0)
            slab_values = blk[at // 2, lax.rem(at, 2)]
            pages[o, s] = jnp.where(
                slab_rows < limit, slab_values.astype(jnp.float32), 0.0
            ).astype(jnp.bfloat16)
    each(lambda d: g_copy(group_peer(d), part).start(), parts)
    own_pages = pltpu.make_async_copy(
        pages.at[part],
        landed_hbm.at[0, :, pl.ds(pl.multiple_of(part * slab, slab), slab), :],
        own_sem,
    )
    own_pages.start()

    each(lambda d: r_copy(peer_at(d), peer_at(d)).wait_recv())
    summed = rrecv[0]
    for t in range(1, n):
        summed = summed + rrecv[t]
    res[role] = summed.astype(jnp.bfloat16)
    swap = pltpu.make_async_remote_copy(
        src_ref=res.at[role],
        dst_ref=res.at[role],
        send_sem=pair_send.at[1],
        recv_sem=pair_recv.at[1],
        device_id={"role": 1 - role},
        device_id_type=MESH,
    )
    swap.start()
    back = pltpu.make_async_remote_copy(
        src_ref=res.at[1 - role],
        dst_ref=res.at[1 - role],
        send_sem=pair_send.at[1],
        recv_sem=pair_recv.at[1],
        device_id={"role": 1 - role},
        device_id_type=MESH,
    )
    back.wait_recv()
    out_ref[...] = res[...]

    own_pages.wait()
    each(lambda d: g_copy(group_peer(d), lax.rem(part + d, parts)).wait_recv(), parts)
    pair.wait_send()
    swap.wait_send()
    each(lambda d: x_copy(peer_at(d), me).wait_send())
    each(lambda d: b_copy(peer_at(d), me).wait_send())
    each(lambda d: a_copy(peer_at(d), me).wait_send())
    each(lambda d: h_copy(peer_at(d), me).wait_send())
    each(lambda d: r_copy(peer_at(d), me).wait_send())
    each(lambda d: g_copy(group_peer(d), part).wait_send(), parts)


def body(
    tokens,
    norm_gain,
    w_query,
    w_keyval,
    w_out,
    kv_cache,
    cache_len,
    prompt_kv,
    block_owner,
    block_tokens,
):
    n = lax.axis_size("tensor")
    tile, width = prompt_kv.shape[2], prompt_kv.shape[3]
    count = prompt_kv.shape[1]
    kvl = w_keyval.shape[1]
    ctx = kv_cache.shape[1]
    rows = 2 * n
    parts = min(n // 2, tile // 16)
    slab = tile // parts
    half_k = CHUNKS * LANES
    pair_width = HEAD + max(HEAD, kvl)
    tok = tokens.reshape(STEPS, 2, CHUNKS, LANES).transpose(1, 0, 2, 3)
    tok = tok.reshape(2, STEPS * CHUNKS, LANES)
    gain = norm_gain.reshape(2, CHUNKS, LANES)
    vmem = pl.BlockSpec(memory_space=pltpu.VMEM)
    smem = pl.BlockSpec(memory_space=pltpu.SMEM)
    anywhere = pl.BlockSpec(memory_space=pl.ANY)
    dma = pltpu.SemaphoreType.DMA
    out, landed = pl.pallas_call(
        functools.partial(kernel, n, parts),
        out_shape=(
            jax.ShapeDtypeStruct((2, STEPS * CHUNKS, LANES), jnp.bfloat16),
            jax.ShapeDtypeStruct((1, CAP, tile, width), jnp.bfloat16),
        ),
        in_specs=[
            vmem,
            vmem,
            anywhere,
            anywhere,
            anywhere,
            anywhere,
            smem,
            anywhere,
            smem,
            smem,
        ],
        out_specs=(vmem, anywhere),
        scratch_shapes=[
            pltpu.VMEM((half_k, HEAD), jnp.bfloat16),
            pltpu.VMEM((half_k, kvl), jnp.bfloat16),
            pltpu.VMEM((HEAD, half_k), jnp.bfloat16),
            pltpu.VMEM((ctx, kv_cache.shape[2]), jnp.bfloat16),
            pltpu.VMEM((n, STEPS * CHUNKS, LANES), jnp.bfloat16),
            pltpu.VMEM((rows * CHUNKS, LANES), jnp.float32),
            pltpu.VMEM((rows, pair_width), jnp.float32),
            pltpu.VMEM((rows, pair_width), jnp.float32),
            pltpu.VMEM((rows * 4, HEAD), jnp.float32),
            pltpu.VMEM((rows * 4, HEAD), jnp.float32),
            pltpu.VMEM((rows * 4, HEAD), jnp.float32),
            pltpu.VMEM((rows * 4, HEAD), jnp.float32),
            pltpu.VMEM((rows * CHUNKS, LANES), jnp.float32),
            pltpu.VMEM((n, STEPS * CHUNKS, LANES), jnp.float32),
            pltpu.VMEM((n, count, slab, width), jnp.bfloat16),
            pltpu.VMEM((parts, CAP, slab, width), jnp.bfloat16),
            pltpu.VMEM((2, STEPS * CHUNKS, LANES), jnp.bfloat16),
            dma((5,)),
            dma,
            dma((2,)),
            dma((2,)),
        ]
        + [dma((n,))] * 10
        + [dma((parts,))] * 2,
        compiler_params=pltpu.CompilerParams(
            collective_id=0, has_side_effects=True, vmem_limit_bytes=48 * 1024 * 1024
        ),
    )(
        tok,
        gain,
        w_query,
        w_keyval,
        w_out,
        kv_cache,
        cache_len,
        prompt_kv,
        block_owner[:, :, 0],
        block_tokens,
    )
    attended = out.reshape(2, STEPS, CHUNKS * LANES).transpose(1, 0, 2)
    return attended.reshape(STEPS, 1, 2 * CHUNKS * LANES), landed


def solution(mesh):
    in_specs = (
        P(None, ("group", "tensor"), None),
        P(),
        P(None, "tensor"),
        P(None, "tensor"),
        P("tensor", None),
        P(("group", "tensor"), None, None),
        P(("group", "tensor")),
        P("role", ("group", "tensor"), None, None),
        P(None, "group", None),
        P(None, "group"),
    )
    out_specs = (P(None, ("group", "tensor"), None), P("role", ("group", "tensor"), None, None))
    return jax.shard_map(body, mesh=mesh, in_specs=in_specs, out_specs=out_specs, check_vma=False)
```

time: 276 us -> 70.1 us (0.25)
  blocking collectives: 193 us -> 0 us
  Pallas kernels: 0 us -> 61.5 us
  starting transfers between devices: 25.7 us -> 0 us
  waiting for transfers between devices: 19.1 us -> 0 us
  matrix products: 13.9 us -> 0 us
  other arithmetic: 8.98 us -> 0 us
  local copies, waits for them, and re-layouts: 12 us -> 6.96 us
    unnamed x1 -> x0, blocking collectives: 129 us -> none
    all_gather x2 -> x0, blocking collectives: 63.8 us -> none  [body(): shard_rows = lax.all_gather(normed, 'tensor', axis=0, tiled=True)]
    pallas_call x0 -> x1, Pallas kernels: none -> 61.5 us  [body(): pl.pallas_call(functools.partial(kernel, n, parts), out_shape=(jax.ShapeD...]
    all_to_all x5 -> x0, starting transfers between devices: 25.7 us -> none  [the longest x2 11 us: body(): lax.all_to_all(projected, 'tensor', split_axis=0, concat_axis=1, tiled=True)]
    all_to_all x5 -> x0, waiting for transfers between devices: 19.1 us -> none  [the longest x2 12.9 us: body(): lax.all_to_all(heads_out, 'tensor', split_axis=1, concat_axis=0, tiled=True)]
    dot_general x14 -> x0, matrix products: 13.9 us -> none  [the longest x2 6 us: body(): jnp.dot(shard_rows, w_keyval, preferred_element_type=jnp.float32)]
    unnamed x27 -> x9, local copies, waits for them, and re-layouts: 8.93 us -> 4.59 us
  transfers between devices with their start and end apart: 5 -> 0, of which waited for: 3 -> 0; matrix products, arithmetic and copies ran while one was open for 6% -> 0% of each run, Pallas kernels for 0% -> 0%
where the time goes in v1:
time: 70.1 us; the launch traced here: 69.8 us
  Pallas kernels  61.5 us (88%)
  local copies, waits for them, and re-layouts  6.96 us (10%)
  between operations  1.3 us (2%)
    pallas_call x1, Pallas kernels, body(): pl.pallas_call(functools.partial(kernel, n, parts), out_shape=(jax.ShapeD...  61.5 us
    unnamed x9, local copies, waits for them, and re-layouts  4.59 us

profile of v1, /device:TPU:0, one launch (start us, length us, event | category | flops | bytes accessed | tf_op | source)
XLA Modules:
  0.0 69.8 jit_solution(9345253402814638242)
XLA Ops:
  1.3 0.9 %copy_bitcast_fusion.1.tok_ref = bf16[2,16,1024]{2,1,0:T(8,128)(2,1)S(1)} fusion(bf16[1,2,16,1024]{3,1,2,0:T(2,128)(2,1)} %bitcast.16), kind=kLoop, calls=%fused_computation.1 | loop fusion | bytes 131072 | tf_op jit(solution)/shard_map/reshape | solution.py:374
  2.1 0.9 %reshape.21.gain_ref = f32[2,8,1024]{2,1,0:T(8,128)S(1)} reshape(f32[16384]{0:T(1024)} %param.11) | data formatting | bytes 131072 | tf_op jit(solution)/shard_map/reshape | solution.py:375
  3.0 0.0 copy-start
  3.0 1.2 %copy-done = bf16[1,512,1024]{2,1,0:T(8,128)(2,1)S(1)} copy-done((bf16[1,512,1024]{2,1,0:T(8,128)(2,1)S(1)}, bf16[1,512,1024]{2,1,0:T(8,128)(2,1)}, u32[]{:S(2)}) %copy-start) | copy-done | bytes 1048600
  4.2 0.0 copy-start.1
  4.2 1.0 %copy-done.1 = bf16[1,2,128,1024]{3,2,1,0:T(8,128)(2,1)S(1)} copy-done((bf16[1,2,128,1024]{3,2,1,0:T(8,128)(2,1)S(1)}, bf16[1,2,128,1024]{3,2,1,0:T(8,128)(2,1)}, u32[]{:S(2)}) %copy-start.1) | copy-done | bytes 524312
  5.3 0.0 copy-start.2
  5.3 0.7 copy-done.2
  5.9 0.0 copy-start.3
  5.9 0.7 copy-done.3
  6.6 61.5 %shard_map.113 = (bf16[2,16,1024]{2,1,0:T(8,128)(2,1)S(1)}, bf16[1,4,128,1024]{3,2,1,0:T(8,128)(2,1)S(1)}) custom-call(bf16[2,16,1024]{2,1,0:T(8,128)(2,1)S(1)} %copy_bitcast_fusion.1.tok_ref, f32[2,8,1024]{2,1,0:T(8,128)S(1)} %reshape.21.gain_ref, bf16[16384,128]{1,0:T(8,128)(2,1)} %wq_hbm.1, bf16[16384,128]{1,0:T(8,128)(2,1)} %wkv_hbm.1, ...), custom_call_target="tpu_custom_call" | custom-call | tf_op jit(solution)/shard_map/pallas_call | solution.py:380
  68.1 0.7 reshape.22
  68.8 1.0 %copy.20 = bf16[1,4,128,1024]{3,2,1,0:T(8,128)(2,1)} copy(bf16[1,4,128,1024]{3,2,1,0:T(8,128)(2,1)S(1)} %get-tuple-element.9) | data formatting | bytes 2097152
Async XLA Ops:
  3.0 1.2 %copy-start = (bf16[1,512,1024]{2,1,0:T(8,128)(2,1)S(1)}, bf16[1,512,1024]{2,1,0:T(8,128)(2,1)}, u32[]{:S(2)}) copy-start(bf16[1,512,1024]{2,1,0:T(8,128)(2,1)} %cache_hbm.1) | copy-start | bytes 3145732
  4.2 1.0 %copy-start.1 = (bf16[1,2,128,1024]{3,2,1,0:T(8,128)(2,1)S(1)}, bf16[1,2,128,1024]{3,2,1,0:T(8,128)(2,1)}, u32[]{:S(2)}) copy-start(bf16[1,2,128,1024]{3,2,1,0:T(8,128)(2,1)} %prompt_hbm.1) | copy-start | bytes 1572868
  5.3 0.7 copy-start.2
  5.9 0.7 copy-start.3

commit v2 on v1

--- a/solution.py
+++ b/solution.py
@@ -14,11 +14,14 @@
 LANES = 1024
 CHUNKS = 8
 MESH = pl.DeviceIdType.MESH
+PIECE = 16
+VMEM_LIMIT = 60 * 1024 * 1024
 
 
 def kernel(
     n,
     parts,
+    pieces,
     tok_ref,
     gain_ref,
     wq_hbm,
@@ -35,6 +38,7 @@
     wkv_v,
     wo_v,
     cache_v,
+    xn,
     xg,
     xf,
     pmine,
@@ -45,8 +49,10 @@
     hrecv,
     rsend,
     rrecv,
-    blk,
-    pages,
+    blk_first,
+    blk_last,
+    pages_first,
+    pages_last,
     res,
     local_sem,
     own_sem,
@@ -72,7 +78,10 @@
     ctx = cache_v.shape[0]
     key_width = KVH * HEAD
     half_k = CHUNKS * LANES
-    slab = blk.shape[2]
+    blks = (blk_first, blk_last)
+    piece = blk_first.shape[2]
+    pages = (pages_first, pages_last)
+    slab = piece * pieces
     nblocks = owner_ref.shape[1]
     part = lax.rem(me, parts)
     base = me - part
@@ -86,9 +95,15 @@
         local(wkv_hbm.at[pl.ds(k0, half_k), :], wkv_v, 1),
         local(cache_hbm.at[0], cache_v, 2),
         local(wo_hbm.at[:, pl.ds(k0, half_k)], wo_v, 3),
+    ] + [
         local(
-            prompt_hbm.at[0, :, pl.ds(pl.multiple_of(part * slab, slab), slab), :], blk.at[me], 4
-        ),
+            prompt_hbm.at[
+                0, :, pl.ds(pl.multiple_of(part * slab + c * piece, piece), piece), :
+            ],
+            blks[c].at[me],
+            4 + c,
+        )
+        for c in range(pieces)
     ]
     for load in loads:
         load.start()
@@ -104,13 +119,16 @@
     pl.semaphore_signal(barrier, inc=1, device_id={"role": 1 - role}, device_id_type=MESH)
     lax.fori_loop(1, n, greet, 0)
 
-    xs = tok_ref[...].astype(jnp.float32).reshape(2, STEPS, CHUNKS, LANES)
-    total = jnp.sum(xs * xs, axis=(0, 2), keepdims=True)
-    total = jnp.sum(total, axis=3, keepdims=True)
-    factor = lax.rsqrt(total[0] * (1.0 / (2 * half_k)) + 1e-05)
-    mine = tok_ref[role].astype(jnp.float32).reshape(STEPS, CHUNKS, LANES)
-    normed = mine * factor * gain_ref[role][None]
-    xg[me] = normed.reshape(STEPS * CHUNKS, LANES).astype(jnp.bfloat16)
+    xs = tok_ref[...].astype(jnp.float32)
+    total = jnp.sum(xs * xs, axis=1, keepdims=True)
+    factor = lax.rsqrt(total * (1.0 / (2 * half_k)) + 1e-05)
+    mine = tok_ref[:, pl.ds(k0, half_k)].astype(jnp.float32)
+    normed = mine * factor * gain_ref[:, pl.ds(k0, half_k)]
+    for c in range(CHUNKS):
+        for s in range(STEPS):
+            at = s * CHUNKS + c
+            xn[at : at + 1, :] = normed[s : s + 1, c * LANES : (c + 1) * LANES]
+    xg[me] = xn[...].astype(jnp.bfloat16)
 
     pl.semaphore_wait(barrier, n)
 
@@ -137,13 +155,15 @@
     def x_copy(peer, slot):
         return remote(xg.at[me], xg.at[slot], x_send.at[peer], x_recv.at[slot], peer)
 
-    def b_copy(peer, slot):
-        at = pl.multiple_of(lax.rem(peer, parts) * slab, slab)
+    def rows_of(p, c):
+        return pl.ds(pl.multiple_of(p * slab + c * piece, piece), piece)
+
+    def b_copy(peer, slot, c):
         return remote(
-            prompt_hbm.at[0, :, pl.ds(at, slab), :],
-            blk.at[slot],
-            b_send.at[peer],
-            b_recv.at[slot],
+            prompt_hbm.at[0, :, rows_of(lax.rem(peer, parts), c), :],
+            blks[c].at[slot],
+            b_send.at[c * n + peer],
+            b_recv.at[c * n + slot],
             peer,
         )
 
@@ -168,18 +188,63 @@
     def group_peer(d):
         return base + lax.rem(part + d, parts)
 
-    def g_copy(peer, slot_part):
+    def g_copy(peer, slot_part, c):
         local_peer = lax.rem(peer, parts)
         return remote(
-            pages.at[local_peer],
-            landed_hbm.at[0, :, pl.ds(pl.multiple_of(slot_part * slab, slab), slab), :],
-            g_send.at[local_peer],
-            g_recv.at[slot_part],
+            pages[c].at[local_peer],
+            landed_hbm.at[0, :, rows_of(slot_part, c), :],
+            g_send.at[c * parts + local_peer],
+            g_recv.at[c * parts + slot_part],
             peer,
         )
 
+    groups = n // parts
+
+    def peer_of(other, k):
+        return lax.rem(me // parts + other, groups) * parts + lax.rem(part + k, parts)
+
+    def blocks_out(c):
+        if c >= pieces:
+            return
+        for k in range(parts):
+            for other in range(groups - 1, -1, -1):
+                if k + other > 0:
+                    b_copy(peer_of(other, k), me, c).start()
+
+    def own_pages(c):
+        return pltpu.make_async_copy(
+            pages[c].at[part], landed_hbm.at[0, :, rows_of(part, c), :], own_sem.at[c]
+        )
+
+    def pack_blocks(c):
+        loads[4 + c].wait()
+        each(lambda d: b_copy(peer_at(d), peer_at(d), c).wait_recv())
+        slab_rows = lax.broadcasted_iota(jnp.int32, (piece, 1), 0) + (part * slab + c * piece)
+        for o in range(parts):
+            wanted = base + o
+
+            def scan(j, carry):
+                hits, found = carry[0], carry[1:]
+                hit = owner_ref[role, j] == wanted
+                found = tuple(
+                    jnp.where(hit & (hits == s), j, found[s]) for s in range(CAP)
+                )
+                return (hits + jnp.where(hit, 1, 0),) + found
+
+            zero = jnp.int32(0)
+            scanned = lax.fori_loop(0, nblocks, scan, (zero,) * (1 + CAP))
+            for s in range(CAP):
+                at = scanned[1 + s]
+                limit = jnp.where(scanned[0] > s, count_ref[role, at], 0)
+                slab_values = blks[c][at // 2, lax.rem(at, 2)]
+                pages[c][o, s] = jnp.where(
+                    slab_rows < limit, slab_values.astype(jnp.float32), 0.0
+                ).astype(jnp.bfloat16)
+        each(lambda d: g_copy(group_peer(d), part, c).start(), parts)
+        own_pages(c).start()
+
     each(lambda d: x_copy(peer_at(d), me).start())
-    each(lambda d: b_copy(peer_at(d), me).start())
+    blocks_out(0)
 
     loads[0].wait()
     loads[1].wait()
@@ -214,6 +279,7 @@
     asend[spread, :] = proj
     asend[spread_next, :] = kv_proj
     each(lambda d: a_copy(peer_at(d), me).start())
+    blocks_out(1)
     block_of(arecv, me, 8)[...] = block_of(asend, me, 8)[...]
     loads[2].wait()
     each(lambda d: a_copy(peer_at(d), peer_at(d)).wait_recv())
@@ -267,6 +333,8 @@
 
     hsend[spread, :] = heads_out
     each(lambda d: h_copy(peer_at(d), me).start())
+    if pieces > 1:
+        pack_blocks(0)
     block_of(hrecv, me, 8)[...] = block_of(hsend, me, 8)[...]
     loads[3].wait()
     each(lambda d: h_copy(peer_at(d), peer_at(d)).wait_recv())
@@ -280,36 +348,7 @@
     each(lambda d: r_copy(peer_at(d), me).start())
     rrecv[me] = block_of(rsend, me, 16)[...]
 
-    loads[4].wait()
-    each(lambda d: b_copy(peer_at(d), peer_at(d)).wait_recv())
-    slab_rows = lax.broadcasted_iota(jnp.int32, (slab, 1), 0) + part * slab
-    for o in range(parts):
-        wanted = base + o
-
-        def scan(j, carry):
-            hits, found = carry[0], carry[1:]
-            hit = owner_ref[role, j] == wanted
-            found = tuple(
-                jnp.where(hit & (hits == s), j, found[s]) for s in range(CAP)
-            )
-            return (hits + jnp.where(hit, 1, 0),) + found
-
-        zero = jnp.int32(0)
-        scanned = lax.fori_loop(0, nblocks, scan, (zero,) * (1 + CAP))
-        for s in range(CAP):
-            at = scanned[1 + s]
-            limit = jnp.where(scanned[0] > s, count_ref[role, at], 0)
-            slab_values = blk[at // 2, lax.rem(at, 2)]
-            pages[o, s] = jnp.where(
-                slab_rows < limit, slab_values.astype(jnp.float32), 0.0
-            ).astype(jnp.bfloat16)
-    each(lambda d: g_copy(group_peer(d), part).start(), parts)
-    own_pages = pltpu.make_async_copy(
-        pages.at[part],
-        landed_hbm.at[0, :, pl.ds(pl.multiple_of(part * slab, slab), slab), :],
-        own_sem,
-    )
-    own_pages.start()
+    pack_blocks(pieces - 1)
 
     each(lambda d: r_copy(peer_at(d), peer_at(d)).wait_recv())
     summed = rrecv[0]
@@ -336,16 +375,19 @@
     back.wait_recv()
     out_ref[...] = res[...]
 
-    own_pages.wait()
-    each(lambda d: g_copy(group_peer(d), lax.rem(part + d, parts)).wait_recv(), parts)
+    for c in range(pieces):
+        own_pages(c).wait()
+        each(
+            lambda d, c=c: g_copy(group_peer(d), lax.rem(part + d, parts), c).wait_recv(), parts
+        )
+        each(lambda d, c=c: b_copy(peer_at(d), me, c).wait_send())
+        each(lambda d, c=c: g_copy(group_peer(d), part, c).wait_send(), parts)
     pair.wait_send()
     swap.wait_send()
     each(lambda d: x_copy(peer_at(d), me).wait_send())
-    each(lambda d: b_copy(peer_at(d), me).wait_send())
     each(lambda d: a_copy(peer_at(d), me).wait_send())
     each(lambda d: h_copy(peer_at(d), me).wait_send())
     each(lambda d: r_copy(peer_at(d), me).wait_send())
-    each(lambda d: g_copy(group_peer(d), part).wait_send(), parts)
 
 
 def body(
@@ -368,17 +410,17 @@
     rows = 2 * n
     parts = min(n // 2, tile // 16)
     slab = tile // parts
+    pieces = 2 if slab % (2 * PIECE) == 0 else 1
     half_k = CHUNKS * LANES
     pair_width = HEAD + max(HEAD, kvl)
-    tok = tokens.reshape(STEPS, 2, CHUNKS, LANES).transpose(1, 0, 2, 3)
-    tok = tok.reshape(2, STEPS * CHUNKS, LANES)
-    gain = norm_gain.reshape(2, CHUNKS, LANES)
+    tok = tokens.reshape(STEPS, 2 * half_k)
+    gain = norm_gain.reshape(1, 2 * half_k)
     vmem = pl.BlockSpec(memory_space=pltpu.VMEM)
     smem = pl.BlockSpec(memory_space=pltpu.SMEM)
     anywhere = pl.BlockSpec(memory_space=pl.ANY)
     dma = pltpu.SemaphoreType.DMA
     out, landed = pl.pallas_call(
-        functools.partial(kernel, n, parts),
+        functools.partial(kernel, n, parts, pieces),
         out_shape=(
             jax.ShapeDtypeStruct((2, STEPS * CHUNKS, LANES), jnp.bfloat16),
             jax.ShapeDtypeStruct((1, CAP, tile, width), jnp.bfloat16),
@@ -401,6 +443,7 @@
             pltpu.VMEM((half_k, kvl), jnp.bfloat16),
             pltpu.VMEM((HEAD, half_k), jnp.bfloat16),
             pltpu.VMEM((ctx, kv_cache.shape[2]), jnp.bfloat16),
+            pltpu.VMEM((STEPS * CHUNKS, LANES), jnp.float32),
             pltpu.VMEM((n, STEPS * CHUNKS, LANES), jnp.bfloat16),
             pltpu.VMEM((rows * CHUNKS, LANES), jnp.float32),
             pltpu.VMEM((rows, pair_width), jnp.float32),
@@ -411,18 +454,22 @@
             pltpu.VMEM((rows * 4, HEAD), jnp.float32),
             pltpu.VMEM((rows * CHUNKS, LANES), jnp.float32),
             pltpu.VMEM((n, STEPS * CHUNKS, LANES), jnp.float32),
-            pltpu.VMEM((n, count, slab, width), jnp.bfloat16),
-            pltpu.VMEM((parts, CAP, slab, width), jnp.bfloat16),
+            pltpu.VMEM((n, count, slab // pieces, width), jnp.bfloat16),
+            pltpu.VMEM((n, count, slab // pieces, width), jnp.bfloat16),
+            pltpu.VMEM((parts, CAP, slab // pieces, width), jnp.bfloat16),
+            pltpu.VMEM((parts, CAP, slab // pieces, width), jnp.bfloat16),
             pltpu.VMEM((2, STEPS * CHUNKS, LANES), jnp.bfloat16),
-            dma((5,)),
-            dma,
+            dma((6,)),
+            dma((2,)),
             dma((2,)),
             dma((2,)),
         ]
-        + [dma((n,))] * 10
-        + [dma((parts,))] * 2,
+        + [dma((n,))] * 2
+        + [dma((pieces * n,))] * 2
+        + [dma((n,))] * 6
+        + [dma((pieces * parts,))] * 2,
         compiler_params=pltpu.CompilerParams(
-            collective_id=0, has_side_effects=True, vmem_limit_bytes=48 * 1024 * 1024
+            collective_id=0, has_side_effects=True, vmem_limit_bytes=VMEM_LIMIT
         ),
     )(
         tok,

time: 70.1 us -> 61.2 us (0.87)
  Pallas kernels: 61.5 us -> 55.9 us
  local copies, waits for them, and re-layouts: 6.96 us -> 3.76 us
    pallas_call x1, Pallas kernels: 61.5 us -> 55.9 us  [body(): pl.pallas_call(functools.partial(kernel, n, parts, pieces), out_shape=(ja...]
    unnamed x9 -> x1, local copies, waits for them, and re-layouts: 4.59 us -> 2.26 us
    reshape x2 -> x0, local copies, waits for them, and re-layouts: 1.71 us -> none  [the longest x1 0.86 us: body(): gain = norm_gain.reshape(2, CHUNKS, LANES)]
    reshape x1, local copies, waits for them, and re-layouts: 0.66 us -> 1.5 us  [body(): attended = out.reshape(2, STEPS, CHUNKS * LANES).transpose(1, 0, 2)]
where the time goes in v2:
time: 61.2 us; the launch traced here: 61 us
  Pallas kernels  55.9 us (91%)
  local copies, waits for them, and re-layouts  3.76 us (6%)
  between operations  1.29 us (2%)
    pallas_call x1, Pallas kernels, body(): pl.pallas_call(functools.partial(kernel, n, parts, pieces), out_shape=(ja...  55.9 us
    unnamed x1, local copies, waits for them, and re-layouts  2.26 us
    reshape x1, local copies, waits for them, and re-layouts, body(): attended = out.reshape(2, STEPS, CHUNKS * LANES).transpose(1, 0, 2)  1.5 us

profile of v2, /device:TPU:0, one launch (start us, length us, event | category | flops | bytes accessed | tf_op | source)
XLA Modules:
  0.0 61.0 jit_solution(17883709448228014876)
XLA Ops:
  1.3 55.9 %shard_map.113 = (bf16[2,16,1024]{2,1,0:T(8,128)(2,1)}, bf16[1,4,128,1024]{3,2,1,0:T(8,128)(2,1)}) custom-call(bf16[2,16384]{1,0:T(2,128)(2,1)} %bitcast.6, f32[1,16384]{1,0:T(1,128)} %bitcast.7, bf16[16384,128]{1,0:T(8,128)(2,1)} %wq_hbm.1, bf16[16384,128]{1,0:T(8,128)(2,1)} %wkv_hbm.1, bf16[128,16384]{1,0:T(8,128)(2,1)} %wo_hbm.1, ...), custom_call_target="tpu_custom_call" | custom-call | tf_op jit(solution)/shard_map/pallas_call | solution.py:422
  57.2 1.5 %reshape.18 = bf16[2,2,8192]{2,1,0:T(2,128)(2,1)} reshape(bf16[2,16,1024]{2,1,0:T(8,128)(2,1)} %get-tuple-element.4) | data formatting | bytes 131072 | tf_op jit(solution)/shard_map/reshape | solution.py:486
  58.7 2.3 %copy.15 = bf16[1,4,128,1024]{3,2,1,0:T(8,128)(2,1)} copy(bf16[1,4,128,1024]{3,2,1,0:T(8,128)(2,1)} %get-tuple-element.9) | data formatting | bytes 2097152
